TPU v7x, 256 devices: a whole 4x4x8 slice. The times are simulated.
256 devices in a mesh: blk: 64 (over x, z, core), kv: 4 (over y).
Axes of the slice: x: 4, y: 4, z: 8, core: 2. Of those that a mesh axis runs over, the one named last changes fastest.
Arguments:
- queries: bfloat16 [8192, 128, 128], P(('blk', 'kv')), may hold values from -30 to 30
- cache_keys: bfloat16 [131072, 8, 128], P('blk', 'kv'), may hold values from -6 to 6
- cache_values: bfloat16 [131072, 8, 128], P('blk', 'kv'), may hold values from -48 to 48
- new_keys: bfloat16 [8192, 8, 128], P(('blk', 'kv')), may hold values from -6 to 6
- new_values: bfloat16 [8192, 8, 128], P(('blk', 'kv')), may hold values from -48 to 48
- counts: int32 [64], P('blk'), may hold values from 129 to 2048, as said below
Outputs:
- attended: bfloat16 [8192, 128, 128], P(('blk', 'kv'))
- logsum: float32 [8192, 128], P(('blk', 'kv'))
Inputs may be any that keep to these rules, and one draw needn't show every extreme that they name: Segment b's live rows are its first counts[b] rows; some segment has all 2048 live.
All inputs are finite; a program needn't handle non-finite values.
Results may differ from a plain program's by a relative error of at most 0.015.
Values may be sent and summed in bfloat16 or wider, within the bound.
A program may use at most 64 MiB of HBM per device.

v0:
```python
import math

import jax
import jax.numpy as jnp
from jax import lax
from jax.sharding import PartitionSpec as P

SPAN = 3


MASKED = -1e30


def passed_along(block, axis, distance):
    devices = range(lax.axis_size(axis))
    route = [((i - distance) % len(devices), i) for i in devices]
    return lax.ppermute(block, axis, route)


def for_sending(value):
    return jax.tree.map(lambda a: a.astype(jnp.bfloat16) if a.dtype == jnp.float32 else a, value)


def absorb(carried, query_heads, key_block, value_block, offset):
    acc_old, top_old, sum_old = carried
    scores = jnp.einsum(
        "qghd,kgd->qghk", query_heads, key_block, preferred_element_type=jnp.float32
    )
    scores = scores * (1.0 / math.sqrt(query_heads.shape[-1])) + offset
    highest = jnp.maximum(top_old, jnp.max(scores, axis=-1))
    rescale = jnp.exp(top_old - highest)
    weights = jnp.exp(scores - highest[..., None])
    sum_new = sum_old * rescale + jnp.sum(weights, axis=-1)
    acc_new = acc_old * rescale[..., None] + jnp.einsum(
        "qghk,kgd->qghd",
        weights.astype(jnp.bfloat16),
        value_block,
        preferred_element_type=jnp.float32,
    )
    return (acc_new, highest, sum_new)


def fold_segment(carried, query_heads, seg_keys, seg_values, live_count):
    block_rows = min(512, seg_keys.shape[0])
    passes = (live_count + block_rows - 1) // block_rows

    def visit(position, running):
        first_row = position * block_rows
        key_block = lax.dynamic_slice_in_dim(seg_keys, first_row, block_rows, 0)
        value_block = lax.dynamic_slice_in_dim(seg_values, first_row, block_rows, 0)
        usable = first_row + jnp.arange(block_rows, dtype=jnp.int32) < live_count
        offset = jnp.where(usable, 0.0, MASKED).astype(jnp.float32)
        return absorb(running, query_heads, key_block, value_block, offset[None, None, None, :])

    return lax.fori_loop(0, passes, visit, carried)


def fold_recent(carried, query_heads, recent_keys, recent_values):
    tok_rows = recent_keys.shape[0]
    block_rows = min(512, tok_rows)
    query_pos = jnp.arange(tok_rows, dtype=jnp.int32)

    def visit(position, running):
        first_row = position * block_rows
        allowed = (first_row + jnp.arange(block_rows, dtype=jnp.int32))[None, :] <= query_pos[
            :, None
        ]
        offset = jnp.where(allowed, 0.0, MASKED).astype(jnp.float32)
        return absorb(running, query_heads, recent_keys, recent_values, offset[:, None, None, :])

    return lax.fori_loop(0, tok_rows // block_rows, visit, carried)


def body(queries, cache_keys, cache_values, new_keys, new_values, counts):
    turn_queries, recent_keys, recent_values = (
        lax.all_to_all(queries, "kv", split_axis=1, concat_axis=0, tiled=True),
        lax.all_to_all(new_keys, "kv", split_axis=1, concat_axis=0, tiled=True),
        lax.all_to_all(new_values, "kv", split_axis=1, concat_axis=0, tiled=True),
    )
    tok_rows = turn_queries.shape[0]
    head_count = turn_queries.shape[1]
    head_width = turn_queries.shape[2]
    kv_local = cache_keys.shape[1]
    grouped = turn_queries.reshape(tok_rows, kv_local, head_count // kv_local, head_width)
    initial = (
        jnp.zeros(grouped.shape, jnp.float32),
        jnp.full(grouped.shape[:3], MASKED, jnp.float32),
        jnp.zeros(grouped.shape[:3], jnp.float32),
    )
    started = fold_recent(initial, grouped, recent_keys, recent_values)
    live_count = counts[0]
    running = fold_segment(started, grouped, cache_keys, cache_values, live_count)
    traveler = grouped
    for stride in range(1, SPAN):
        traveler = passed_along(traveler, "blk", -1)
        running = passed_along(running, "blk", -1)
        running = fold_segment(running, traveler, cache_keys, cache_values, live_count)
    running = jax.tree.map(
        lambda part, own: part.astype(own.dtype),
        passed_along(for_sending(running), "blk", SPAN - 1),
        running,
    )
    accum, highest, totals = running
    attended = (
        (accum / totals[..., None]).astype(jnp.bfloat16).reshape(tok_rows, head_count, head_width)
    )
    logsum = (highest + jnp.log(totals)).reshape(tok_rows, head_count)
    seq_output = lax.all_to_all(attended, "kv", split_axis=0, concat_axis=1, tiled=True)
    seq_logsum = lax.all_to_all(logsum, "kv", split_axis=0, concat_axis=1, tiled=True)
    return (seq_output, seq_logsum)


def solution(mesh):
    in_specs = (
        P(("blk", "kv"), None, None),
        P("blk", "kv", None),
        P("blk", "kv", None),
        P(("blk", "kv"), None, None),
        P(("blk", "kv"), None, None),
        P("blk"),
    )
    out_specs = (P(("blk", "kv"), None, None), P(("blk", "kv"), None))
    return jax.shard_map(body, mesh=mesh, in_specs=in_specs, out_specs=out_specs, check_vma=False)
```

profile of v0, /device:TPU:6, one launch (start us, length us, event | category | flops | bytes accessed | tf_op | source)
XLA Modules:
  0.0 282.3 jit_solution(14566199416100457138)
XLA Ops:
  2.1 4.5 %all-to-all-start = ((bf16[32,8,128]{2,0,1:T(8,128)(2,1)}), bf16[32,8,128]{2,0,1:T(8,128)(2,1)S(1)}, u32[]{:S(2)}, u32[]{:S(2)}) async-start(bf16[32,8,128]{2,0,1:T(8,128)(2,1)} %copy.79), calls=%async_computation | async-start | bytes 131072 | tf_op jit(solution)/shard_map/all_to_all | solution.py:77
  8.0 4.2 %all-to-all-done = bf16[32,8,128]{2,0,1:T(8,128)(2,1)S(1)} async-done(((bf16[32,8,128]{2,0,1:T(8,128)(2,1)}), bf16[32,8,128]{2,0,1:T(8,128)(2,1)S(1)}, u32[]{:S(2)}, u32[]{:S(2)}) %all-to-all-start) | async-done | bytes 65568 | tf_op jit(solution)/shard_map/all_to_all | solution.py:77
  12.2 3.3 %all-to-all-start.2 = ((bf16[32,8,128]{2,0,1:T(8,128)(2,1)}), bf16[32,8,128]{2,0,1:T(8,128)(2,1)S(1)}, u32[]{:S(2)}, u32[]{:S(2)}) async-start(bf16[32,8,128]{2,0,1:T(8,128)(2,1)} %copy.83), calls=%async_computation.2 | async-start | bytes 131072 | tf_op jit(solution)/shard_map/all_to_all | solution.py:78
  15.5 2.9 %copy.81 = bf16[32,128,128]{2,0,1:T(8,128)(2,1)} copy(bf16[32,128,128]{2,1,0:T(8,128)(2,1)} %param.12) | data formatting | bytes 2097152 | tf_op args[0]
  18.4 2.7 all-to-all-done.2
  21.1 3.5 %all-to-all-start.1 = ((bf16[32,128,128]{2,0,1:T(8,128)(2,1)}), bf16[32,128,128]{2,0,1:T(8,128)(2,1)S(1)}, u32[]{:S(2)}, u32[]{:S(2)}) async-start(bf16[32,128,128]{2,0,1:T(8,128)(2,1)} %copy.81), calls=%async_computation.1 | async-start | bytes 2097152 | tf_op jit(solution)/shard_map/all_to_all | solution.py:76
  25.3 2.3 copy.87
  27.6 3.7 %copy.88 = bf16[2048,2,128]{0,2,1:T(8,128)(2,1)} copy(bf16[2048,2,128]{2,1,0:T(2,128)(2,1)} %param.14) | data formatting | bytes 2097152 | tf_op jit(solution)/shard_map/while | solution.py:55
  31.4 6.0 %all-to-all-done.1 = bf16[32,128,128]{2,0,1:T(8,128)(2,1)S(1)} async-done(((bf16[32,128,128]{2,0,1:T(8,128)(2,1)}), bf16[32,128,128]{2,0,1:T(8,128)(2,1)S(1)}, u32[]{:S(2)}, u32[]{:S(2)}) %all-to-all-start.1) | async-done | bytes 1048608 | tf_op jit(solution)/shard_map/all_to_all | solution.py:76
  38.4 2.1 bitcast_add_fusion.3
  42.4 8.3 %while.17 = (s32[]{:T(128)}, f32[128,2,16,128]{0,3,2,1:T(8,128)S(1)}, f32[128,2,16]{0,2,1:T(8,128)S(1)}, f32[128,2,16]{0,2,1:T(8,128)S(1)}, s32[]{:T(128)}, /*in...) while((s32[]{:T(128)}, ...), condition=%wide.region_5.6_spmd, body=%wide.region_2.5_spmd.sunk | while | flops 1097868800 | bytes 31203516 | solution.py:55
  43.1 2.2 bitcast_reduce_fusion.6
  45.3 2.0 fusion.80
  47.4 3.3 %bitcast_add_fusion.8 = f32[128,2,16,128]{0,3,2,1:T(8,128)S(1)} fusion(f32[128,2,16,128]{0,3,2,1:T(8,128)S(1)} %get-tuple-element.599, f32[2,512,128,16]{2,1,3,0:T(8,128)S(1)} %get-tuple-element.555, f32[128,2,16]{0,2,1:T(8,128)S(1)} %max.29, f32[512]{0:T(512)S(1)} %fusion.79, f32[128,2,16]{0,2,1:T(8,128)S(1)} %get-tuple-element.557, ...), kind=kOutput, calls=%fused_computation.7.clone.1 | convolution fusion | flops 546308096 | bytes 12879876 | tf_op jit(solution)/shard_map/while/body/qghk,kgd->qghd/dot_general | solution.py:34
  50.7 26.7 %collective-permute-start = (f32[128,2,16,128]{0,3,2,1:T(8,128)S(1)}, f32[128,2,16,128]{0,3,2,1:T(8,128)}, u32[]{:S(2)}, u32[]{:S(2)}) collective-permute-start(f32[128,2,16,128]{0,3,2,1:T(8,128)S(1)} %get-tuple-element.179), channel_id=1, source_target_pairs={{4,0},{8,4},{12,8},{16,12},{20,16},{24,20},{28,24},{32,28},{36,32}... | collective-permute-start | bytes 6291464 | tf_op jit(solution)/shard_map/ppermute | solution.py:17
  77.3 4.5 %collective-permute-start.3 = (bf16[128,2,16,128]{3,0,2,1:T(8,128)(2,1)S(1)}, bf16[128,2,16,128]{3,0,2,1:T(8,128)(2,1)}, u32[]{:S(2)}, u32[]{:S(2)}) collective-permute-start(bf16[128,2,16,128]{3,0,2,1:T(8,128)(2,1)S(1)} %get-tuple-element.704), channel_id=1, source_target_pairs={{4,0},{8,4},{12,8},{16,12},{20,16},{24,20},{28,24},{32,28},{36,32}... | collective-permute-start | bytes 3145736 | tf_op jit(solution)/shard_map/ppermute | solution.py:17
  82.0 30.3 %collective-permute-done.1 = f32[128,2,16]{0,2,1:T(8,128)S(1)} collective-permute-done((f32[128,2,16]{0,2,1:T(8,128)S(1)}, f32[128,2,16]{0,2,1:T(8,128)S(1)}, u32[]{:S(2)}, u32[]{:S(2)}) %collective-permute-start.1) | collective-permute-done | bytes 16416 | tf_op jit(solution)/shard_map/ppermute | solution.py:17
  112.5 10.5 %while.50 = (s32[]{:T(128)}, f32[128,2,16,128]{0,3,2,1:T(8,128)}, f32[128,2,16]{0,2,1:T(8,128)S(1)}, f32[128,2,16]{0,2,1:T(8,128)S(1)}, s32[]{:T(128)}, /*index=...) while((s32[]{:T(128)}, f32[128,2,16,128]{0,3,2,1:T(8,128)}, ...), condition=%wide.region_9.10_spmd, body=%wide.region_6.9_spmd.sunk | while | flops 1097868800 | bytes 31203516 | solution.py:55
  113.2 2.6 bitcast_reduce_fusion.7
  115.8 2.0 fusion.85
  117.8 5.2 %bitcast_add_fusion.9 = f32[128,2,16,128]{0,3,2,1:T(8,128)} fusion(f32[128,2,16,128]{0,3,2,1:T(8,128)} %get-tuple-element.638, f32[2,512,128,16]{2,1,3,0:T(8,128)S(1)} %get-tuple-element.568, f32[128,2,16]{0,2,1:T(8,128)S(1)} %max.30, f32[512]{0:T(512)S(1)} %fusion.84, f32[128,2,16]{0,2,1:T(8,128)S(1)} %get-tuple-element.570, ...), kind=kOutput, calls=%fused_computation.27.clone.1 | convolution fusion | flops 546308096 | bytes 12879876 | tf_op jit(solution)/shard_map/while/body/qghk,kgd->qghd/dot_general | solution.py:34
  123.0 35.5 %collective-permute-start.4 = (f32[128,2,16,128]{0,3,2,1:T(8,128)}, f32[128,2,16,128]{0,3,2,1:T(8,128)S(1)}, u32[]{:S(2)}, u32[]{:S(2)}) collective-permute-start(f32[128,2,16,128]{0,3,2,1:T(8,128)} %get-tuple-element.182), channel_id=1, source_target_pairs={{4,0},{8,4},{12,8},{16,12},{20,16},{24,20},{28,24},{32,28},{36,32}... | collective-permute-start | bytes 6291464 | tf_op jit(solution)/shard_map/ppermute | solution.py:17
  160.9 32.7 %collective-permute-done.7 = bf16[128,2,16,128]{3,0,2,1:T(8,128)(2,1)S(1)} collective-permute-done((bf16[128,2,16,128]{3,0,2,1:T(8,128)(2,1)}, bf16[128,2,16,128]{3,0,2,1:T(8,128)(2,1)S(1)}, u32[]{:S(2)}, u32[]{:S(2)}) %collective-permute-start.7) | collective-permute-done | bytes 1048608 | tf_op jit(solution)/shard_map/ppermute | solution.py:17
  193.8 8.3 %while.51 = (s32[]{:T(128)}, f32[128,2,16,128]{0,3,2,1:T(8,128)S(1)}, f32[128,2,16]{0,2,1:T(8,128)S(1)}, f32[128,2,16]{0,2,1:T(8,128)S(1)}, s32[]{:T(128)}, /*in...) while((s32[]{:T(128)}, ...), condition=%wide.region_13.14_spmd, body=%wide.region_10.13_spmd.sunk | while | flops 1097868800 | bytes 31203516 | solution.py:55
  194.5 2.2 bitcast_reduce_fusion.8
  198.8 3.3 %bitcast_add_fusion.10 = f32[128,2,16,128]{0,3,2,1:T(8,128)S(1)} fusion(f32[128,2,16,128]{0,3,2,1:T(8,128)S(1)} %get-tuple-element.677, f32[2,512,128,16]{2,1,3,0:T(8,128)S(1)} %get-tuple-element.581, f32[128,2,16]{0,2,1:T(8,128)S(1)} %max.31, f32[512]{0:T(512)S(1)} %fusion.89, f32[128,2,16]{0,2,1:T(8,128)S(1)} %get-tuple-element.583, ...), kind=kOutput, calls=%fused_computation.47.clone.1 | convolution fusion | flops 546308096 | bytes 12879876 | tf_op jit(solution)/shard_map/while/body/qghk,kgd->qghd/dot_general | solution.py:34
  202.3 21.2 %collective-permute-start.8 = (bf16[128,2,16,128]{0,3,2,1:T(8,128)(2,1)S(1)}, bf16[128,2,16,128]{0,3,2,1:T(8,128)(2,1)S(1)}, u32[]{:S(2)}, u32[]{:S(2)}) collective-permute-start(bf16[128,2,16,128]{0,3,2,1:T(8,128)(2,1)S(1)} %convert_element_type.35), channel_id=1, source_target_pairs={{248,0},{252,4},{0,8},{4,12},{8,16},{12,20},{16,24},{20,28},{24,32... | collective-permute-start | bytes 3145736 | tf_op jit(solution)/shard_map/ppermute | solution.py:17
  223.7 28.6 %collective-permute-done.10 = bf16[128,2,16]{0,2,1:T(8,128)(2,1)S(1)} collective-permute-done((bf16[128,2,16]{0,2,1:T(8,128)(2,1)S(1)}, bf16[128,2,16]{0,2,1:T(8,128)(2,1)S(1)}, u32[]{:S(2)}, u32[]{:S(2)}) %collective-permute-start.10) | collective-permute-done | bytes 8224 | tf_op jit(solution)/shard_map/ppermute | solution.py:17
  253.4 3.3 %all-to-all-start.4 = ((f32[4,1,1024]{2,1,0:T(1,128)}), f32[4,1,1024]{2,1,0:T(1,128)S(1)}, u32[]{:S(2)}, u32[]{:S(2)}) async-start(f32[4,1,1024]{2,1,0:T(1,128)} %reshape.70), calls=%async_computation.4 | async-start | bytes 32768 | tf_op jit(solution)/shard_map/all_to_all | solution.py:109
  258.7 3.3 %all-to-all-done.4 = f32[4,1,1024]{2,1,0:T(1,128)S(1)} async-done(((f32[4,1,1024]{2,1,0:T(1,128)}), f32[4,1,1024]{2,1,0:T(1,128)S(1)}, u32[]{:S(2)}, u32[]{:S(2)}) %all-to-all-start.4) | async-done | bytes 16416 | tf_op jit(solution)/shard_map/all_to_all | solution.py:109
  262.0 3.5 %all-to-all-start.3 = ((bf16[128,32,128]{2,1,0:T(8,128)(2,1)}), bf16[128,32,128]{2,1,0:T(8,128)(2,1)S(1)}, u32[]{:S(2)}, u32[]{:S(2)}) async-start(bf16[128,32,128]{2,1,0:T(8,128)(2,1)} %bitcast.35), calls=%async_computation.3 | async-start | bytes 2097152 | tf_op jit(solution)/shard_map/all_to_all | solution.py:108
  267.5 13.7 %all-to-all-done.3 = bf16[128,32,128]{2,1,0:T(8,128)(2,1)S(1)} async-done(((bf16[128,32,128]{2,1,0:T(8,128)(2,1)}), bf16[128,32,128]{2,1,0:T(8,128)(2,1)S(1)}, u32[]{:S(2)}, u32[]{:S(2)}) %all-to-all-start.3) | async-done | bytes 1048608 | tf_op jit(solution)/shard_map/all_to_all | solution.py:108
  (55 shorter events, 19.5 us)
Async XLA Ops:
  2.1 10.1 %all-to-all-start = ((bf16[32,8,128]{2,0,1:T(8,128)(2,1)}), bf16[32,8,128]{2,0,1:T(8,128)(2,1)S(1)}, u32[]{:S(2)}, u32[]{:S(2)}) async-start(bf16[32,8,128]{2,0,1:T(8,128)(2,1)} %copy.79), calls=%async_computation | async-start | bytes 131072 | tf_op jit(solution)/shard_map/all_to_all | solution.py:77
  12.2 8.9 %all-to-all-start.2 = ((bf16[32,8,128]{2,0,1:T(8,128)(2,1)}), bf16[32,8,128]{2,0,1:T(8,128)(2,1)S(1)}, u32[]{:S(2)}, u32[]{:S(2)}) async-start(bf16[32,8,128]{2,0,1:T(8,128)(2,1)} %copy.83), calls=%async_computation.2 | async-start | bytes 131072 | tf_op jit(solution)/shard_map/all_to_all | solution.py:78
  21.1 16.3 %all-to-all-start.1 = ((bf16[32,128,128]{2,0,1:T(8,128)(2,1)}), bf16[32,128,128]{2,0,1:T(8,128)(2,1)S(1)}, u32[]{:S(2)}, u32[]{:S(2)}) async-start(bf16[32,128,128]{2,0,1:T(8,128)(2,1)} %copy.81), calls=%async_computation.1 | async-start | bytes 2097152 | tf_op jit(solution)/shard_map/all_to_all | solution.py:76
  50.7 61.8 %collective-permute-start = (f32[128,2,16,128]{0,3,2,1:T(8,128)S(1)}, f32[128,2,16,128]{0,3,2,1:T(8,128)}, u32[]{:S(2)}, u32[]{:S(2)}) collective-permute-start(f32[128,2,16,128]{0,3,2,1:T(8,128)S(1)} %get-tuple-element.179), channel_id=1, source_target_pairs={{4,0},{8,4},{12,8},{16,12},{20,16},{24,20},{28,24},{32,28},{36,32}... | collective-permute-start | bytes 6291464 | tf_op jit(solution)/shard_map/ppermute | solution.py:17
  77.3 35.1 %collective-permute-start.3 = (bf16[128,2,16,128]{3,0,2,1:T(8,128)(2,1)S(1)}, bf16[128,2,16,128]{3,0,2,1:T(8,128)(2,1)}, u32[]{:S(2)}, u32[]{:S(2)}) collective-permute-start(bf16[128,2,16,128]{3,0,2,1:T(8,128)(2,1)S(1)} %get-tuple-element.704), channel_id=1, source_target_pairs={{4,0},{8,4},{12,8},{16,12},{20,16},{24,20},{28,24},{32,28},{36,32}... | collective-permute-start | bytes 3145736 | tf_op jit(solution)/shard_map/ppermute | solution.py:17
  81.8 30.5 %collective-permute-start.1 = (f32[128,2,16]{0,2,1:T(8,128)S(1)}, f32[128,2,16]{0,2,1:T(8,128)S(1)}, u32[]{:S(2)}, u32[]{:S(2)}) collective-permute-start(f32[128,2,16]{0,2,1:T(8,128)S(1)} %get-tuple-element.180), channel_id=1, source_target_pairs={{4,0},{8,4},{12,8},{16,12},{20,16},{24,20},{28,24},{32,28},{36,32}... | collective-permute-start | bytes 49160 | tf_op jit(solution)/shard_map/ppermute | solution.py:17
  81.9 30.6 %collective-permute-start.2 = (f32[128,2,16]{0,2,1:T(8,128)S(1)}, f32[128,2,16]{0,2,1:T(8,128)S(1)}, u32[]{:S(2)}, u32[]{:S(2)}) collective-permute-start(f32[128,2,16]{0,2,1:T(8,128)S(1)} %get-tuple-element.181), channel_id=1, source_target_pairs={{4,0},{8,4},{12,8},{16,12},{20,16},{24,20},{28,24},{32,28},{36,32}... | collective-permute-start | bytes 49160 | tf_op jit(solution)/shard_map/ppermute | solution.py:17
  123.0 70.9 %collective-permute-start.4 = (f32[128,2,16,128]{0,3,2,1:T(8,128)}, f32[128,2,16,128]{0,3,2,1:T(8,128)S(1)}, u32[]{:S(2)}, u32[]{:S(2)}) collective-permute-start(f32[128,2,16,128]{0,3,2,1:T(8,128)} %get-tuple-element.182), channel_id=1, source_target_pairs={{4,0},{8,4},{12,8},{16,12},{20,16},{24,20},{28,24},{32,28},{36,32}... | collective-permute-start | bytes 6291464 | tf_op jit(solution)/shard_map/ppermute | solution.py:17
  158.5 35.1 %collective-permute-start.7 = (bf16[128,2,16,128]{3,0,2,1:T(8,128)(2,1)}, bf16[128,2,16,128]{3,0,2,1:T(8,128)(2,1)S(1)}, u32[]{:S(2)}, u32[]{:S(2)}) collective-permute-start(bf16[128,2,16,128]{3,0,2,1:T(8,128)(2,1)} %collective-permute-done.3), channel_id=1, source_target_pairs={{4,0},{8,4},{12,8},{16,12},{20,16},{24,20},{28,24},{32,28},{36,32}... | collective-permute-start | bytes 3145736 | tf_op jit(solution)/shard_map/ppermute | solution.py:17
  158.9 34.8 %collective-permute-start.5 = (f32[128,2,16]{0,2,1:T(8,128)S(1)}, f32[128,2,16]{0,2,1:T(8,128)S(1)}, u32[]{:S(2)}, u32[]{:S(2)}) collective-permute-start(f32[128,2,16]{0,2,1:T(8,128)S(1)} %get-tuple-element.183), channel_id=1, source_target_pairs={{4,0},{8,4},{12,8},{16,12},{20,16},{24,20},{28,24},{32,28},{36,32}... | collective-permute-start | bytes 49160 | tf_op jit(solution)/shard_map/ppermute | solution.py:17
  160.9 33.0 %collective-permute-start.6 = (f32[128,2,16]{0,2,1:T(8,128)S(1)}, f32[128,2,16]{0,2,1:T(8,128)S(1)}, u32[]{:S(2)}, u32[]{:S(2)}) collective-permute-start(f32[128,2,16]{0,2,1:T(8,128)S(1)} %get-tuple-element.184), channel_id=1, source_target_pairs={{4,0},{8,4},{12,8},{16,12},{20,16},{24,20},{28,24},{32,28},{36,32}... | collective-permute-start | bytes 49160 | tf_op jit(solution)/shard_map/ppermute | solution.py:17
  202.3 54.4 %collective-permute-start.8 = (bf16[128,2,16,128]{0,3,2,1:T(8,128)(2,1)S(1)}, bf16[128,2,16,128]{0,3,2,1:T(8,128)(2,1)S(1)}, u32[]{:S(2)}, u32[]{:S(2)}) collective-permute-start(bf16[128,2,16,128]{0,3,2,1:T(8,128)(2,1)S(1)} %convert_element_type.35), channel_id=1, source_target_pairs={{248,0},{252,4},{0,8},{4,12},{8,16},{12,20},{16,24},{20,28},{24,32... | collective-permute-start | bytes 3145736 | tf_op jit(solution)/shard_map/ppermute | solution.py:17
  223.5 28.8 %collective-permute-start.10 = (bf16[128,2,16]{0,2,1:T(8,128)(2,1)S(1)}, bf16[128,2,16]{0,2,1:T(8,128)(2,1)S(1)}, u32[]{:S(2)}, u32[]{:S(2)}) collective-permute-start(bf16[128,2,16]{0,2,1:T(8,128)(2,1)S(1)} %convert_element_type.40), channel_id=1, source_target_pairs={{248,0},{252,4},{0,8},{4,12},{8,16},{12,20},{16,24},{20,28},{24,32... | collective-permute-start | bytes 24584 | tf_op jit(solution)/shard_map/ppermute | solution.py:17
  223.6 28.9 %collective-permute-start.9 = (bf16[128,2,16]{0,2,1:T(8,128)(2,1)S(1)}, bf16[128,2,16]{0,2,1:T(8,128)(2,1)S(1)}, u32[]{:S(2)}, u32[]{:S(2)}) collective-permute-start(bf16[128,2,16]{0,2,1:T(8,128)(2,1)S(1)} %convert_element_type.37), channel_id=1, source_target_pairs={{248,0},{252,4},{0,8},{4,12},{8,16},{12,20},{16,24},{20,28},{24,32... | collective-permute-start | bytes 24584 | tf_op jit(solution)/shard_map/ppermute | solution.py:17
  253.4 8.6 %all-to-all-start.4 = ((f32[4,1,1024]{2,1,0:T(1,128)}), f32[4,1,1024]{2,1,0:T(1,128)S(1)}, u32[]{:S(2)}, u32[]{:S(2)}) async-start(f32[4,1,1024]{2,1,0:T(1,128)} %reshape.70), calls=%async_computation.4 | async-start | bytes 32768 | tf_op jit(solution)/shard_map/all_to_all | solution.py:109
  262.0 19.2 %all-to-all-start.3 = ((bf16[128,32,128]{2,1,0:T(8,128)(2,1)}), bf16[128,32,128]{2,1,0:T(8,128)(2,1)S(1)}, u32[]{:S(2)}, u32[]{:S(2)}) async-start(bf16[128,32,128]{2,1,0:T(8,128)(2,1)} %bitcast.35), calls=%async_computation.3 | async-start | bytes 2097152 | tf_op jit(solution)/shard_map/all_to_all | solution.py:108
where the time goes:
time: 284 us; the launch traced here: 282 us
  waiting for transfers between devices  122 us (43%)
  starting transfers between devices  109 us (38%)
  matrix products  21.3 us (8%)
  local copies, waits for them, and re-layouts  19 us (7%)
  other arithmetic  9.62 us (3%)
    ppermute x11, waiting for transfers between devices, passed_along(): return lax.ppermute(block, axis, route)  92.2 us
    ppermute x11, starting transfers between devices, passed_along(): return lax.ppermute(block, axis, route)  90.6 us
    dot_general x4, matrix products, absorb(): jnp.einsum('qghk,kgd->qghd', weights.astype(jnp.bfloat16), value_block, p...  13.8 us
    all_to_all x1, waiting for transfers between devices, body(): lax.all_to_all(attended, 'kv', split_axis=0, concat_axis=1, tiled=True)  13.7 us
    while x3, local copies, waits for them, and re-layouts, fold_segment(): return lax.fori_loop(0, passes, visit, carried)  7.98 us
    dot_general x4, matrix products, absorb(): jnp.einsum('qghd,kgd->qghk', query_heads, key_block, preferred_element_ty...  7.51 us
    unnamed x5, local copies, waits for them, and re-layouts  6.62 us
    reduce_sum x4, other arithmetic, absorb(): sum_new = sum_old * rescale + jnp.sum(weights, axis=-1)  6.41 us
  transfers between devices with their start and end apart: 16, of which 12 were waited for; matrix products, arithmetic and copies ran while one was open for 5% of the time, Pallas kernels for 0%

commit v1 on v0

v1 whole, which is shorter than its diff:
```python
import functools
import math

import jax
import jax.numpy as jnp
from jax import lax
from jax.experimental import pallas as pl
from jax.experimental.pallas import tpu as pltpu
from jax.sharding import PartitionSpec as P

MESH = pl.DeviceIdType.MESH
LOG2E = math.log2(math.e)
NEG = -1e30
KC = 256
EXT = 16

ORDER = (
    ("X", 0), ("Z", 0), ("Y", 1), ("X", 1), ("Z", 1), ("X", 3),
    ("Z", 3), ("X", 2), ("Z", 2), ("Y", 3), ("Y", 2), ("Y", 0),
)
FINISH = {3: [(0, 0)], 5: [(1, 1)], 6: [(0, 1)], 8: [(0, 3)], 9: [(1, 3)], 10: [(0, 2), (1, 2)], 11: [(1, 0)]}
FORWARD = {0: [], 1: [1, 3], 5: [2]}


def look(position, values):
    result = jnp.int32(values[-1])
    for i in reversed(range(len(values) - 1)):
        result = jnp.where(position == i, jnp.int32(values[i]), result)
    return result


def dot(a, b, ca, cb):
    return lax.dot_general(a, b, (((ca,), (cb,)), ((), ())), preferred_element_type=jnp.float32)


def pack_log(value):
    hi = value.astype(jnp.bfloat16).astype(jnp.float32)
    mid = (value - hi).astype(jnp.bfloat16).astype(jnp.float32)
    low = value - hi - mid
    row = lax.broadcasted_iota(jnp.int32, (EXT, value.shape[1]), 0)
    packed = jnp.where(row == 0, hi, jnp.where(row == 1, mid, jnp.where(row == 2, low, 0.0)))
    return packed.astype(jnp.bfloat16)


def unpack_log(rows):
    wide = rows.astype(jnp.float32)
    return wide[0:1] + wide[1:2] + wide[2:3]


def kernel(
    nb, ny,
    counts, q_in, ck_in, cv_in, nk_in, nv_in,
    o_out, lse_out,
    raw_k, raw_v, wide, k_buf, v_buf, k_send, v_send, qall, new_raw, new_send, new_buf,
    s0, s1, m0, m1, p0, p1, acc_a, acc_b, res, part_in, o_stage, lse_stage,
    load_sem, q_send, q_recv, z_send, f_send, n_send, n_recv, x_send, x_recv,
    r_send, r_recv, o_send, o_recv, l_send, l_recv,
):
    cap = k_buf.shape[1]
    tok, grp, hd = qall.shape[1:]
    rows = tok * grp
    half = rows // 2
    scale = LOG2E / math.sqrt(hd)

    b = lax.axis_index("blk")
    y = lax.axis_index("kv")
    g = lax.rem(b, 2)
    chip0 = b - g
    prev0 = lax.rem(chip0 + nb - 2, nb)
    next0 = lax.rem(chip0 + 2, nb)
    other = (chip0 + 1 - g, y)

    def peer(dj, di):
        return lax.rem(g + di, 2), lax.rem(y + dj, ny)

    peers = [(dj, di) for dj in range(ny) for di in range(2) if (dj, di) != (0, 0)]

    load_k = pltpu.make_async_copy(ck_in, raw_k, load_sem.at[0])
    load_v = pltpu.make_async_copy(cv_in, raw_v, load_sem.at[1])
    load_nk = pltpu.make_async_copy(nk_in, new_raw.at[0], load_sem.at[2])
    load_nv = pltpu.make_async_copy(nv_in, new_raw.at[1], load_sem.at[3])
    load_k.start()
    load_nk.start()
    load_nv.start()
    load_v.start()

    def heads_of(gg, yy):
        return pl.ds(pl.multiple_of((2 * yy + gg) * grp, grp), grp)

    load_q = pltpu.make_async_copy(q_in.at[:, heads_of(g, y), :], qall.at[g], q_recv.at[g])
    load_q.start()

    barrier = pltpu.get_barrier_semaphore()
    for dj, di in peers:
        gg, yy = peer(dj, di)
        pl.semaphore_signal(barrier, inc=1, device_id=(chip0 + gg, yy), device_id_type=MESH)
    for base in (prev0, next0):
        for i in range(2):
            pl.semaphore_signal(barrier, inc=1, device_id=(base + i, y), device_id_type=MESH)
    pl.semaphore_wait(barrier, len(peers) + 4)

    def q_copy(n, dj, di):
        gg, yy = peer(dj, di)
        slot = ((ny - dj) % ny) * 2 + g
        return pltpu.make_async_remote_copy(
            src_ref=q_in.at[:, heads_of(gg, yy), :], dst_ref=qall.at[slot],
            send_sem=q_send.at[n], recv_sem=q_recv.at[slot],
            device_id=(chip0 + gg, yy), device_id_type=MESH,
        )

    def z_copy(gg):
        slot = 2 * ny + g
        return pltpu.make_async_remote_copy(
            src_ref=q_in.at[:, heads_of(gg, y), :], dst_ref=qall.at[slot],
            send_sem=z_send.at[gg], recv_sem=q_recv.at[slot],
            device_id=(prev0 + gg, y), device_id_type=MESH,
        )

    def forward_copy(slot):
        return pltpu.make_async_remote_copy(
            src_ref=qall.at[slot], dst_ref=qall.at[2 * ny + slot],
            send_sem=f_send.at[slot], recv_sem=q_recv.at[2 * ny + slot],
            device_id=(prev0 + g, y), device_id_type=MESH,
        )

    def q_wait(slot):
        pltpu.make_async_remote_copy(
            src_ref=qall.at[slot], dst_ref=qall.at[slot],
            send_sem=f_send.at[0], recv_sem=q_recv.at[slot],
            device_id=other, device_id_type=MESH,
        ).wait_recv()

    order = {}
    for n, pair in enumerate(peers):
        order[pair] = n
    send_order = sorted(peers, key=lambda pair: (0, ny - 1, 1, 2)[pair[0]] if ny == 4 else pair[0])
    send_order = [(0, 1)] + [pair for pair in send_order if pair != (0, 1)]
    q_copy(order[(0, 1)], 0, 1).start()
    z_copy(0).start()
    z_copy(1).start()
    for pair in send_order[1:]:
        q_copy(order[pair], *pair).start()

    live = counts[0]

    def split_keys(head):
        x = wide[pl.ds(head, cap, stride=2), :]
        index = lax.broadcasted_iota(jnp.int32, (cap, hd), 0)
        return jnp.where(index < live, x, x[0:1, :]).astype(jnp.bfloat16)

    def split_values(head, store):
        for c in range(cap // 128):
            x = wide[pl.ds(c * 256 + head, 128, stride=2), :]
            column = lax.broadcasted_iota(jnp.int32, (hd, 128), 1) + c * 128
            store(c, jnp.where(column < live, x.T, 0.0).astype(jnp.bfloat16))

    def live_rows():
        row = lax.broadcasted_iota(jnp.int32, (EXT, cap), 0)
        column = lax.broadcasted_iota(jnp.int32, (EXT, cap), 1)
        return jnp.where((row == 0) & (column < live), 1.0, 0.0).astype(jnp.bfloat16)

    def x_copy(n):
        src, dst = ((k_send, k_buf), (v_send, v_buf))[n]
        return pltpu.make_async_remote_copy(
            src_ref=src, dst_ref=dst.at[g], send_sem=x_send.at[n], recv_sem=x_recv.at[n],
            device_id=other, device_id_type=MESH,
        )

    load_k.wait()
    wide[0 : cap * 2, :] = raw_k[...].astype(jnp.float32)
    k_send[...] = split_keys(1 - g)
    x_copy(0).start()
    k_buf[g] = split_keys(g)

    load_v.wait()
    wide[0 : cap * 2, :] = raw_v[...].astype(jnp.float32)

    def to_send(c, x):
        v_send[0:hd, c * 128 : (c + 1) * 128] = x

    def to_own(c, x):
        v_buf[g, 0:hd, c * 128 : (c + 1) * 128] = x

    split_values(1 - g, to_send)
    v_send[hd : hd + EXT, :] = live_rows()
    x_copy(1).start()
    split_values(g, to_own)
    v_buf[g, hd : hd + EXT, :] = live_rows()

    nh = new_raw.shape[1] // tok

    def n_copy(n, dj, di):
        gg, yy = peer(dj, di)
        slot = ((ny - dj) % ny) * 2 + g
        return pltpu.make_async_remote_copy(
            src_ref=new_send.at[n], dst_ref=new_buf.at[slot],
            send_sem=n_send.at[n], recv_sem=n_recv.at[slot],
            device_id=(chip0 + gg, yy), device_id_type=MESH,
        )

    load_nk.wait()
    load_nv.wait()
    for kind in range(2):
        wide[pl.ds(kind * tok * nh, tok * nh), :] = new_raw[kind].astype(jnp.float32)
    for n, (dj, di) in enumerate(peers):
        gg, yy = peer(dj, di)
        for kind in range(2):
            new_send[n, kind] = wide[pl.ds(kind * tok * nh + 2 * yy + gg, tok, stride=nh), :].astype(jnp.bfloat16)
        n_copy(n, dj, di).start()
    for kind in range(2):
        new_buf[g, kind] = wide[pl.ds(kind * tok * nh + 2 * y + g, tok, stride=nh), :].astype(jnp.bfloat16)

    def scores(qa, t, seg, kk):
        qq = qall[qa, t * (tok // 2) : (t + 1) * (tok // 2)].reshape(half, hd)
        return dot(k_buf[seg, kk, :], qq, 1, 1)

    def fold(chunk):
        return jnp.max(chunk.reshape(KC // 8, 8, half), axis=0)

    def first(qa, seg, s_ref, m_ref):
        for t in range(2):
            cols = slice(t * half, (t + 1) * half)
            top = None
            for c in range(cap // KC):
                kk = slice(c * KC, (c + 1) * KC)
                s = scores(qa, t, seg, kk)
                s_ref[kk, cols] = s
                top = fold(s) if top is None else jnp.maximum(top, fold(s))
            m_ref[:, cols] = jnp.broadcast_to(jnp.max(top, axis=0, keepdims=True), (8, half))

    def both(qa, seg, s_new, m_new, s_old, m_old, seg_old, acc):
        for t in range(2):
            cols = slice(t * half, (t + 1) * half)
            p_ref = (p0, p1)[t]
            old = m_old[0:1, cols]
            top = None
            for c in range(cap // KC):
                kk = slice(c * KC, (c + 1) * KC)
                s = scores(qa, t, seg, kk)
                s_new[kk, cols] = s
                top = fold(s) if top is None else jnp.maximum(top, fold(s))
                p_ref[kk, :] = jnp.exp2((s_old[kk, cols] - old) * scale).astype(jnp.bfloat16)
            m_new[:, cols] = jnp.broadcast_to(jnp.max(top, axis=0, keepdims=True), (8, half))
            acc[:, cols] = dot(v_buf[seg_old], p_ref[...], 1, 0)

    def log2(x):
        return jnp.log(x) * LOG2E

    steps = len(ORDER)
    kinds = [k for k, _ in ORDER]
    sources = [j for _, j in ORDER]
    qa_of = [{"X": 2 * j, "Y": 2 * j + 1, "Z": 2 * (ny + j)}[k] for k, j in ORDER]
    qb_of = [{"X": 2 * (ny + j) + 1, "Y": 2 * j + 1, "Z": 2 * (ny + j)}[k] for k, j in ORDER]
    part_of = [{"X": 2 * j + 1, "Y": 0, "Z": 2 * j}[k] for k, j in ORDER]
    finish = [e for p in range(steps) for e in FINISH.get(p, [])]
    ends = [sum(len(FINISH.get(r, [])) for r in range(p + 1)) for p in range(steps)]
    begins = [0] + ends[:-1]
    final_slot = [2 * j + i for i, j in finish]
    final_res = [2 * ORDER.index(("X", j)) if i == 0 else 2 * ORDER.index(("Y", j)) + 1 for i, j in finish]

    def r_copy(p):
        slot = look(p, part_of)
        return pltpu.make_async_remote_copy(
            src_ref=res.at[2 * p + 1], dst_ref=part_in.at[slot],
            send_sem=r_send.at[slot], recv_sem=r_recv.at[slot],
            device_id=(next0 + g, y), device_id_type=MESH,
        )

    def r_wait(slot):
        pltpu.make_async_remote_copy(
            src_ref=part_in.at[slot], dst_ref=part_in.at[slot],
            send_sem=r_send.at[slot], recv_sem=r_recv.at[slot],
            device_id=other, device_id_type=MESH,
        ).wait_recv()

    own_heads = heads_of(g, y)
    own_block = 2 * y + g

    def o_remote(slot, tile, yy):
        return pltpu.make_async_remote_copy(
            src_ref=o_stage.at[slot], dst_ref=o_out.at[:, own_heads, :],
            send_sem=o_send.at[slot], recv_sem=o_recv.at[own_block],
            device_id=(chip0 + tile, yy), device_id_type=MESH,
        )

    def l_remote(slot, tile, yy):
        return pltpu.make_async_remote_copy(
            src_ref=lse_stage.at[slot], dst_ref=lse_out.at[own_block],
            send_sem=l_send.at[slot], recv_sem=l_recv.at[own_block],
            device_id=(chip0 + tile, yy), device_id_type=MESH,
        )

    def o_local(slot):
        return pltpu.make_async_copy(o_stage.at[slot], o_out.at[:, own_heads, :], o_send.at[slot])

    def l_local(slot):
        return pltpu.make_async_copy(lse_stage.at[slot], lse_out.at[own_block], l_send.at[slot])

    def finish_block(e, carry):
        slot = look(e, final_slot)
        src = look(e, final_res)
        tile = lax.rem(slot, 2)
        yy = lax.rem(y + lax.div(slot, 2), ny)
        r_wait(slot)
        queries = qall[slot].reshape(rows, hd)
        keys = jnp.concatenate([new_buf[2 * j + tile, 0] for j in range(ny)], axis=0)
        vals = jnp.concatenate([new_buf[2 * j + tile, 1] for j in range(ny)], axis=0)
        s = dot(keys, queries, 1, 1)
        key_row = lax.broadcasted_iota(jnp.int32, s.shape, 0)
        key_pos = lax.rem(lax.div(key_row, tok) + y, ny) * tok + lax.rem(key_row, tok)
        token = lax.div(lax.broadcasted_iota(jnp.int32, s.shape, 1), grp) + yy * tok
        s = jnp.where(key_pos <= token, s, NEG)
        top = jnp.max(s, axis=0, keepdims=True)
        p = jnp.exp2((s - top) * scale)
        total = jnp.sum(p, axis=0, keepdims=True)
        mix = dot(vals, p.astype(jnp.bfloat16), 0, 0)
        e0 = top * scale
        e1 = unpack_log(res[src, hd : hd + EXT, :])
        e2 = unpack_log(part_in[slot, hd : hd + EXT, :])
        high = jnp.maximum(e0, jnp.maximum(e1, e2))
        w0 = jnp.exp2(e0 - high)
        w1 = jnp.exp2(e1 - high)
        w2 = jnp.exp2(e2 - high)
        whole = w0 * total + w1 + w2
        inv = 1.0 / whole
        out = mix * (w0 * inv)
        out += res[src, 0:hd, :].astype(jnp.float32) * (w1 * inv)
        out += part_in[slot, 0:hd, :].astype(jnp.float32) * (w2 * inv)
        o_stage[slot] = out.T.astype(jnp.bfloat16).reshape(tok, grp, hd)
        lse_stage[slot] = jnp.broadcast_to((high + log2(whole)) * (1.0 / LOG2E), (8, rows))
        mine = slot == g

        @pl.when(mine)
        def _():
            o_local(slot).start()
            l_local(slot).start()

        @pl.when(jnp.logical_not(mine))
        def _():
            o_remote(slot, tile, yy).start()
            l_remote(slot, tile, yy).start()

        return carry

    load_q.wait()
    q_wait(1 - g)
    x_copy(0).wait_recv()
    first(qa_of[0], 0, s0, m0)
    q_wait(qb_of[0])
    for dj, di in peers:
        slot = 2 * dj + lax.rem(g + di, 2)
        pltpu.make_async_remote_copy(
            src_ref=new_buf.at[slot], dst_ref=new_buf.at[slot],
            send_sem=n_send.at[0], recv_sem=n_recv.at[slot], device_id=other, device_id_type=MESH,
        ).wait_recv()
    x_copy(1).wait_recv()

    def step(p, carry):
        later = lax.rem(p + 1, steps)
        qb = look(p, qb_of)
        qa_later = look(later, qa_of)
        kind_x = look(p, [int(k == "X") for k in kinds])
        top_a = m0[0:1, :] * scale
        both(qb, 1, s1, m1, s0, m0, 0, acc_a)
        total_a = acc_a[hd : hd + 1, :]
        ea = top_a + log2(total_a)
        res[2 * p, 0:hd, :] = (acc_a[0:hd, :] * (1.0 / total_a)).astype(jnp.bfloat16)
        res[2 * p, hd : hd + EXT, :] = pack_log(ea)

        for at, js in FORWARD.items():
            if js:

                @pl.when(p == at)
                def _(js=js):
                    for j in js:
                        for i in (1, 0):
                            q_wait(2 * j + i)
                            forward_copy(2 * j + i).start()

        for at in range(steps - 1):
            kind, j = ORDER[at + 1]
            if kind in "XZ":

                @pl.when(p == at)
                def _(slot=qb_of[at + 1]):
                    q_wait(slot)

        top_b = m1[0:1, :] * scale
        both(qa_later, 0, s0, m0, s1, m1, 1, acc_b)
        total_b = acc_b[hd : hd + 1, :]
        eb = top_b + log2(total_b)
        ea = ea + jnp.where(kind_x == 1, NEG, 0.0)
        high = jnp.maximum(ea, eb)
        wa = jnp.exp2(ea - high)
        wb = jnp.exp2(eb - high)
        whole = wa + wb
        merged = acc_a[0:hd, :] * (wa / (whole * total_a)) + acc_b[0:hd, :] * (wb / (whole * total_b))
        res[2 * p + 1, 0:hd, :] = merged.astype(jnp.bfloat16)
        res[2 * p + 1, hd : hd + EXT, :] = pack_log(high + log2(whole))

        @pl.when(look(p, [int(k != "Y") for k in kinds]) == 1)
        def _():
            r_copy(p).start()

        lax.fori_loop(look(p, begins), look(p, ends), finish_block, 0)
        return carry

    lax.fori_loop(0, steps, step, 0)

    for n, (dj, di) in enumerate(peers):
        q_copy(n, dj, di).wait_send()
        n_copy(n, dj, di).wait_send()
    for i in range(2):
        z_copy(i).wait_send()
        x_copy(i).wait_send()
    for slot in range(2, 2 * ny):
        forward_copy(slot).wait_send()
    for p, (kind, j) in enumerate(ORDER):
        if kind != "Y":
            r_copy(p).wait_send()
    for slot in range(2 * ny):
        tile, yy = slot % 2, lax.rem(y + slot // 2, ny)
        if slot < 2:

            @pl.when(g == slot)
            def _():
                o_local(slot).wait()
                l_local(slot).wait()

            @pl.when(g != slot)
            def _():
                o_remote(slot, tile, yy).wait_send()
                l_remote(slot, tile, yy).wait_send()
        else:
            o_remote(slot, tile, yy).wait_send()
            l_remote(slot, tile, yy).wait_send()
    for dj, di in peers:
        gg, yy = peer(dj, di)
        block = 2 * yy + gg
        pltpu.make_async_remote_copy(
            src_ref=o_stage.at[0], dst_ref=o_out.at[:, heads_of(gg, yy), :],
            send_sem=o_send.at[0], recv_sem=o_recv.at[block], device_id=other, device_id_type=MESH,
        ).wait_recv()
        pltpu.make_async_remote_copy(
            src_ref=lse_stage.at[0], dst_ref=lse_out.at[block],
            send_sem=l_send.at[0], recv_sem=l_recv.at[block], device_id=other, device_id_type=MESH,
        ).wait_recv()


def body(queries, cache_keys, cache_values, new_keys, new_values, counts):
    nb, ny = lax.axis_size("blk"), lax.axis_size("kv")
    tok, nq, hd = queries.shape
    cap, kvl, _ = cache_keys.shape
    nh = new_keys.shape[1]
    grp = nq // nh
    rows = tok * grp
    bf16, f32 = jnp.bfloat16, jnp.float32
    vmem, dma = pltpu.VMEM, pltpu.SemaphoreType.DMA
    any_space = pl.BlockSpec(memory_space=pl.ANY)
    steps, own = len(ORDER), 2 * ny
    attended, lse = pl.pallas_call(
        functools.partial(kernel, nb, ny),
        out_shape=(
            jax.ShapeDtypeStruct((tok, nq, hd), bf16),
            jax.ShapeDtypeStruct((own, 8, rows), f32),
        ),
        in_specs=[pl.BlockSpec(memory_space=pltpu.SMEM)] + [any_space] * 5,
        out_specs=(any_space, any_space),
        scratch_shapes=[
            vmem((cap * kvl, hd), bf16), vmem((cap * kvl, hd), bf16), vmem((cap * kvl + 16, hd), f32),
            vmem((2, cap, hd), bf16), vmem((2, hd + EXT, cap), bf16),
            vmem((cap, hd), bf16), vmem((hd + EXT, cap), bf16),
            vmem((2 * own, tok, grp, hd), bf16),
            vmem((2, tok * nh, hd), bf16), vmem((own - 1, 2, tok, hd), bf16), vmem((own, 2, tok, hd), bf16),
            vmem((cap, rows), f32), vmem((cap, rows), f32), vmem((8, rows), f32), vmem((8, rows), f32),
            vmem((cap, rows // 2), bf16), vmem((cap, rows // 2), bf16),
            vmem((hd + EXT, rows), f32), vmem((hd + EXT, rows), f32),
            vmem((2 * steps, hd + EXT, rows), bf16), vmem((own, hd + EXT, rows), bf16),
            vmem((own, tok, grp, hd), bf16), vmem((own, 8, rows), f32),
            dma((4,)), dma((own - 1,)), dma((2 * own,)), dma((2,)), dma((own,)), dma((own - 1,)), dma((own,)),
            dma((2,)), dma((2,)), dma((own,)), dma((own,)), dma((own,)), dma((own,)), dma((own,)), dma((own,)),
        ],
        compiler_params=pltpu.CompilerParams(
            collective_id=0, has_side_effects=True, vmem_limit_bytes=56 * 2**20
        ),
    )(
        counts, queries, cache_keys.reshape(cap * kvl, hd), cache_values.reshape(cap * kvl, hd),
        new_keys.reshape(tok * nh, hd), new_values.reshape(tok * nh, hd),
    )
    logsum = lse[:, 0, :].reshape(own, tok, grp).transpose(1, 0, 2).reshape(tok, nq)
    return attended, logsum


def solution(mesh):
    in_specs = (
        P(("blk", "kv"), None, None),
        P("blk", "kv", None),
        P("blk", "kv", None),
        P(("blk", "kv"), None, None),
        P(("blk", "kv"), None, None),
        P("blk"),
    )
    out_specs = (P(("blk", "kv"), None, None), P(("blk", "kv"), None))
    return jax.shard_map(body, mesh=mesh, in_specs=in_specs, out_specs=out_specs, check_vma=False)
```

time: 284 us -> 77.2 us (0.27)
  the two profiles are of different devices: /device:TPU:6 before, /device:TPU:1 now
where the time goes in v1:
time: 77.2 us; the launch traced here: 77.1 us
  Pallas kernels  71.7 us (93%)
  local copies, waits for them, and re-layouts  4.12 us (5%)
  between operations  1.3 us (2%)
    pallas_call x1, Pallas kernels, body(): pl.pallas_call(functools.partial(kernel, nb, ny), out_shape=(jax.ShapeDty...  71.7 us
    unnamed x2, local copies, waits for them, and re-layouts  3 us

profile of v1, /device:TPU:1, one launch (start us, length us, event | category | flops | bytes accessed | tf_op | source)
XLA Modules:
  0.0 77.1 jit_solution(9346629998586337260)
XLA Ops:
  1.3 71.7 %shard_map.77 = (bf16[32,128,128]{2,1,0:T(8,128)(2,1)}, f32[8,8,512]{2,1,0:T(8,128)}) custom-call(s32[1]{0:T(128)S(6)} %copy.12.counts, bf16[32,128,128]{2,1,0:T(8,128)(2,1)} %q_in.1, bf16[4096,128]{1,0:T(8,128)(2,1)} %bitcast.6, bf16[4096,128]{1,0:T(8,128)(2,1)} %bitcast.7, bf16[256,128]{1,0:T(8,128)(2,1)} %bitcast.10, bf16[256,128]{1,0:T(8,128)(2,1)} %bitcast.11), custom_call_target="tpu_custom_call" | custom-call | tf_op jit(solution)/shard_map/pallas_call | solution.py:461
  72.9 0.9 %slice_reduce_fusion = f32[8,512]{1,0:T(8,128)S(1)} fusion(f32[8,8,512]{2,1,0:T(8,128)} %get-tuple-element.5), kind=kLoop, calls=%fused_computation | loop fusion | bytes 32768 | tf_op jit(solution)/shard_map/slice | solution.py:490
  73.9 0.1 reshape_squeeze.3
  74.0 0.1 copy.9
  74.1 0.7 copy.10
  74.8 2.3 %copy.13 = bf16[32,128,128]{2,1,0:T(8,128)(2,1)} copy(bf16[32,128,128]{2,1,0:T(8,128)(2,1)} %get-tuple-element.10) | data formatting | bytes 2097152

commit v2 on v1

--- a/solution.py
+++ b/solution.py
@@ -15,11 +15,12 @@
 EXT = 16
 
 ORDER = (
-    ("X", 0), ("Z", 0), ("Y", 1), ("X", 1), ("Z", 1), ("X", 3),
-    ("Z", 3), ("X", 2), ("Z", 2), ("Y", 3), ("Y", 2), ("Y", 0),
+    ("Y", 0), ("X", 0), ("Y", 1), ("Z", 0), ("X", 1), ("Z", 1),
+    ("X", 2), ("Z", 2), ("Y", 2), ("X", 3), ("Z", 3), ("Y", 3),
 )
-FINISH = {3: [(0, 0)], 5: [(1, 1)], 6: [(0, 1)], 8: [(0, 3)], 9: [(1, 3)], 10: [(0, 2), (1, 2)], 11: [(1, 0)]}
-FORWARD = {0: [], 1: [1, 3], 5: [2]}
+FINISH = {4: (1, 0), 6: (0, 0), 7: (1, 1), 8: (0, 1), 9: (1, 2), 10: (0, 2)}
+FINISH_LAST = ((1, 3), (0, 3))
+FORWARD = {0: (1, 1), 1: (1, 0), 2: (2, 1), 3: (2, 0), 5: (3, 1), 6: (3, 0)}
 
 
 def look(position, values):
@@ -70,10 +71,13 @@
     next0 = lax.rem(chip0 + 2, nb)
     other = (chip0 + 1 - g, y)
 
-    def peer(dj, di):
-        return lax.rem(g + di, 2), lax.rem(y + dj, ny)
-
-    peers = [(dj, di) for dj in range(ny) for di in range(2) if (dj, di) != (0, 0)]
+    peers = [(0, 1 - g)] + [(dj, gg) for dj in range(1, ny) for gg in range(2)]
+
+    def row(dj):
+        return lax.rem(y + dj, ny)
+
+    def source(j):
+        return lax.rem(ny + (1 - 2 * g) * j, ny)
 
     load_k = pltpu.make_async_copy(ck_in, raw_k, load_sem.at[0])
     load_v = pltpu.make_async_copy(cv_in, raw_v, load_sem.at[1])
@@ -90,22 +94,12 @@
     load_q = pltpu.make_async_copy(q_in.at[:, heads_of(g, y), :], qall.at[g], q_recv.at[g])
     load_q.start()
 
-    barrier = pltpu.get_barrier_semaphore()
-    for dj, di in peers:
-        gg, yy = peer(dj, di)
-        pl.semaphore_signal(barrier, inc=1, device_id=(chip0 + gg, yy), device_id_type=MESH)
-    for base in (prev0, next0):
-        for i in range(2):
-            pl.semaphore_signal(barrier, inc=1, device_id=(base + i, y), device_id_type=MESH)
-    pl.semaphore_wait(barrier, len(peers) + 4)
-
-    def q_copy(n, dj, di):
-        gg, yy = peer(dj, di)
+    def q_copy(dj, gg):
         slot = ((ny - dj) % ny) * 2 + g
         return pltpu.make_async_remote_copy(
-            src_ref=q_in.at[:, heads_of(gg, yy), :], dst_ref=qall.at[slot],
-            send_sem=q_send.at[n], recv_sem=q_recv.at[slot],
-            device_id=(chip0 + gg, yy), device_id_type=MESH,
+            src_ref=q_in.at[:, heads_of(gg, row(dj)), :], dst_ref=qall.at[slot],
+            send_sem=q_send.at[2 * dj + gg], recv_sem=q_recv.at[slot],
+            device_id=(chip0 + gg, row(dj)), device_id_type=MESH,
         )
 
     def z_copy(gg):
@@ -130,34 +124,14 @@
             device_id=other, device_id_type=MESH,
         ).wait_recv()
 
-    order = {}
-    for n, pair in enumerate(peers):
-        order[pair] = n
-    send_order = sorted(peers, key=lambda pair: (0, ny - 1, 1, 2)[pair[0]] if ny == 4 else pair[0])
-    send_order = [(0, 1)] + [pair for pair in send_order if pair != (0, 1)]
-    q_copy(order[(0, 1)], 0, 1).start()
-    z_copy(0).start()
-    z_copy(1).start()
-    for pair in send_order[1:]:
-        q_copy(order[pair], *pair).start()
+    barrier = pltpu.get_barrier_semaphore()
+    for dj, gg in peers:
+        pl.semaphore_signal(barrier, inc=1, device_id=(chip0 + gg, row(dj)), device_id_type=MESH)
+    for base in (prev0, next0):
+        for i in range(2):
+            pl.semaphore_signal(barrier, inc=1, device_id=(base + i, y), device_id_type=MESH)
 
     live = counts[0]
-
-    def split_keys(head):
-        x = wide[pl.ds(head, cap, stride=2), :]
-        index = lax.broadcasted_iota(jnp.int32, (cap, hd), 0)
-        return jnp.where(index < live, x, x[0:1, :]).astype(jnp.bfloat16)
-
-    def split_values(head, store):
-        for c in range(cap // 128):
-            x = wide[pl.ds(c * 256 + head, 128, stride=2), :]
-            column = lax.broadcasted_iota(jnp.int32, (hd, 128), 1) + c * 128
-            store(c, jnp.where(column < live, x.T, 0.0).astype(jnp.bfloat16))
-
-    def live_rows():
-        row = lax.broadcasted_iota(jnp.int32, (EXT, cap), 0)
-        column = lax.broadcasted_iota(jnp.int32, (EXT, cap), 1)
-        return jnp.where((row == 0) & (column < live), 1.0, 0.0).astype(jnp.bfloat16)
 
     def x_copy(n):
         src, dst = ((k_send, k_buf), (v_send, v_buf))[n]
@@ -167,48 +141,83 @@
         )
 
     load_k.wait()
-    wide[0 : cap * 2, :] = raw_k[...].astype(jnp.float32)
-    k_send[...] = split_keys(1 - g)
-    x_copy(0).start()
-    k_buf[g] = split_keys(g)
-
+    top_rows = raw_k[0:16, :].astype(jnp.float32)
+    first_keys = [jnp.where(head == 0, top_rows[0:1], top_rows[1:2]) for head in (1 - g, g)]
+
+    def split_keys(c, carry):
+        at = pl.multiple_of(c * KC, KC)
+        wide[pl.ds(2 * at, 2 * KC), :] = raw_k[pl.ds(2 * at, 2 * KC), :].astype(jnp.float32)
+        index = lax.broadcasted_iota(jnp.int32, (KC, hd), 0) + at
+        for n, head in enumerate((1 - g, g)):
+            x = wide[pl.ds(2 * at + head, KC, stride=2), :]
+            x = jnp.where(index < live, x, first_keys[n]).astype(jnp.bfloat16)
+            if n == 0:
+                k_send[pl.ds(at, KC), :] = x
+            else:
+                k_buf[g, pl.ds(at, KC), :] = x
+        return carry
+
+    lax.fori_loop(0, cap // KC, split_keys, 0)
     load_v.wait()
-    wide[0 : cap * 2, :] = raw_v[...].astype(jnp.float32)
-
-    def to_send(c, x):
-        v_send[0:hd, c * 128 : (c + 1) * 128] = x
-
-    def to_own(c, x):
-        v_buf[g, 0:hd, c * 128 : (c + 1) * 128] = x
-
-    split_values(1 - g, to_send)
-    v_send[hd : hd + EXT, :] = live_rows()
-    x_copy(1).start()
-    split_values(g, to_own)
-    v_buf[g, hd : hd + EXT, :] = live_rows()
+
+    def split_values(c, carry):
+        at = pl.multiple_of(c * KC, KC)
+        wide[pl.ds(2 * at, 2 * KC), :] = raw_v[pl.ds(2 * at, 2 * KC), :].astype(jnp.float32)
+        column = lax.broadcasted_iota(jnp.int32, (hd, KC), 1) + at
+        mark_row = lax.broadcasted_iota(jnp.int32, (EXT, KC), 0)
+        mark_column = lax.broadcasted_iota(jnp.int32, (EXT, KC), 1) + at
+        marks = jnp.where((mark_row == 0) & (mark_column < live), 1.0, 0.0).astype(jnp.bfloat16)
+        for n, head in enumerate((1 - g, g)):
+            x = wide[pl.ds(2 * at + head, KC, stride=2), :]
+            x = jnp.where(column < live, x.T, 0.0).astype(jnp.bfloat16)
+            if n == 0:
+                v_send[0:hd, pl.ds(at, KC)] = x
+                v_send[hd : hd + EXT, pl.ds(at, KC)] = marks
+            else:
+                v_buf[g, 0:hd, pl.ds(at, KC)] = x
+                v_buf[g, hd : hd + EXT, pl.ds(at, KC)] = marks
+        return carry
+
+    lax.fori_loop(0, cap // KC, split_values, 0)
 
     nh = new_raw.shape[1] // tok
 
-    def n_copy(n, dj, di):
-        gg, yy = peer(dj, di)
+    def n_copy(dj, gg):
         slot = ((ny - dj) % ny) * 2 + g
+        n = 2 * dj + gg
         return pltpu.make_async_remote_copy(
             src_ref=new_send.at[n], dst_ref=new_buf.at[slot],
             send_sem=n_send.at[n], recv_sem=n_recv.at[slot],
-            device_id=(chip0 + gg, yy), device_id_type=MESH,
+            device_id=(chip0 + gg, row(dj)), device_id_type=MESH,
         )
 
     load_nk.wait()
     load_nv.wait()
     for kind in range(2):
-        wide[pl.ds(kind * tok * nh, tok * nh), :] = new_raw[kind].astype(jnp.float32)
-    for n, (dj, di) in enumerate(peers):
-        gg, yy = peer(dj, di)
-        for kind in range(2):
-            new_send[n, kind] = wide[pl.ds(kind * tok * nh + 2 * yy + gg, tok, stride=nh), :].astype(jnp.bfloat16)
-        n_copy(n, dj, di).start()
+        wide[kind * tok * nh : (kind + 1) * tok * nh, :] = new_raw[kind].astype(jnp.float32)
     for kind in range(2):
-        new_buf[g, kind] = wide[pl.ds(kind * tok * nh + 2 * y + g, tok, stride=nh), :].astype(jnp.bfloat16)
+        for dj in range(ny):
+            for gg in range(2):
+                head = 2 * row(dj) + gg
+                x = wide[pl.ds(kind * tok * nh + head, tok, stride=nh), :].astype(jnp.bfloat16)
+                new_send[2 * dj + gg, kind] = x
+        new_buf[g, kind] = new_send[g, kind]
+
+    pl.semaphore_wait(barrier, len(peers) + 4)
+    x_copy(0).start()
+    q_copy(0, 1 - g).start()
+
+    @pl.when(g == 1)
+    def _():
+        z_copy(0).start()
+        z_copy(1).start()
+
+    x_copy(1).start()
+    for dj, gg in peers:
+        n_copy(dj, gg).start()
+
+    q_copy(ny - 1, 0).start()
+    q_copy(1, 1).start()
 
     def scores(qa, t, seg, kk):
         qq = qall[qa, t * (tok // 2) : (t + 1) * (tok // 2)].reshape(half, hd)
@@ -249,17 +258,21 @@
     steps = len(ORDER)
     kinds = [k for k, _ in ORDER]
     sources = [j for _, j in ORDER]
-    qa_of = [{"X": 2 * j, "Y": 2 * j + 1, "Z": 2 * (ny + j)}[k] for k, j in ORDER]
-    qb_of = [{"X": 2 * (ny + j) + 1, "Y": 2 * j + 1, "Z": 2 * (ny + j)}[k] for k, j in ORDER]
-    part_of = [{"X": 2 * j + 1, "Y": 0, "Z": 2 * j}[k] for k, j in ORDER]
-    finish = [e for p in range(steps) for e in FINISH.get(p, [])]
-    ends = [sum(len(FINISH.get(r, [])) for r in range(p + 1)) for p in range(steps)]
-    begins = [0] + ends[:-1]
-    final_slot = [2 * j + i for i, j in finish]
-    final_res = [2 * ORDER.index(("X", j)) if i == 0 else 2 * ORDER.index(("Y", j)) + 1 for i, j in finish]
+    own = 2 * ny
+    base_a = [{"X": 0, "Y": 1, "Z": own}[k] for k in kinds]
+    base_b = [{"X": own + 1, "Y": 1, "Z": own}[k] for k in kinds]
+    part_tile = [int(k == "X") for k in kinds]
+
+    def qa_at(p):
+        return look(p, base_a) + 2 * source(look(p, sources))
+
+    def qb_at(p):
+        return look(p, base_b) + 2 * source(look(p, sources))
+
+    at_steps = [FINISH.get(p, (0, 0)) for p in range(steps)]
 
     def r_copy(p):
-        slot = look(p, part_of)
+        slot = look(p, part_tile) + 2 * source(look(p, sources))
         return pltpu.make_async_remote_copy(
             src_ref=res.at[2 * p + 1], dst_ref=part_in.at[slot],
             send_sem=r_send.at[slot], recv_sem=r_recv.at[slot],
@@ -296,12 +309,12 @@
     def l_local(slot):
         return pltpu.make_async_copy(lse_stage.at[slot], lse_out.at[own_block], l_send.at[slot])
 
-    def finish_block(e, carry):
-        slot = look(e, final_slot)
-        src = look(e, final_res)
+    def slot_of(tile, j):
+        return 2 * source(j) + tile
+
+    def finish_math(slot, src, part, stage):
         tile = lax.rem(slot, 2)
         yy = lax.rem(y + lax.div(slot, 2), ny)
-        r_wait(slot)
         queries = qall[slot].reshape(rows, hd)
         keys = jnp.concatenate([new_buf[2 * j + tile, 0] for j in range(ny)], axis=0)
         vals = jnp.concatenate([new_buf[2 * j + tile, 1] for j in range(ny)], axis=0)
@@ -316,7 +329,7 @@
         mix = dot(vals, p.astype(jnp.bfloat16), 0, 0)
         e0 = top * scale
         e1 = unpack_log(res[src, hd : hd + EXT, :])
-        e2 = unpack_log(part_in[slot, hd : hd + EXT, :])
+        e2 = unpack_log(part_in[part, hd : hd + EXT, :])
         high = jnp.maximum(e0, jnp.maximum(e1, e2))
         w0 = jnp.exp2(e0 - high)
         w1 = jnp.exp2(e1 - high)
@@ -325,9 +338,13 @@
         inv = 1.0 / whole
         out = mix * (w0 * inv)
         out += res[src, 0:hd, :].astype(jnp.float32) * (w1 * inv)
-        out += part_in[slot, 0:hd, :].astype(jnp.float32) * (w2 * inv)
-        o_stage[slot] = out.T.astype(jnp.bfloat16).reshape(tok, grp, hd)
-        lse_stage[slot] = jnp.broadcast_to((high + log2(whole)) * (1.0 / LOG2E), (8, rows))
+        out += part_in[part, 0:hd, :].astype(jnp.float32) * (w2 * inv)
+        o_stage[stage] = out.T.astype(jnp.bfloat16).reshape(tok, grp, hd)
+        lse_stage[stage] = jnp.broadcast_to((high + log2(whole)) * (1.0 / LOG2E), (8, rows))
+
+    def finish_send(slot):
+        tile = lax.rem(slot, 2)
+        yy = lax.rem(y + lax.div(slot, 2), ny)
         mine = slot == g
 
         @pl.when(mine)
@@ -340,53 +357,50 @@
             o_remote(slot, tile, yy).start()
             l_remote(slot, tile, yy).start()
 
-        return carry
+    def state_of(tile, j):
+        return 2 * ORDER.index(("X", j)) if tile == 0 else 2 * ORDER.index(("Y", j)) + 1
 
     load_q.wait()
     q_wait(1 - g)
     x_copy(0).wait_recv()
-    first(qa_of[0], 0, s0, m0)
-    q_wait(qb_of[0])
-    for dj, di in peers:
-        slot = 2 * dj + lax.rem(g + di, 2)
+    first(qa_at(0), 0, s0, m0)
+
+    @pl.when(g == 0)
+    def _():
+        z_copy(0).start()
+        z_copy(1).start()
+
+    for dj in range(2, ny - 1):
+        for gg in range(2):
+            q_copy(dj, gg).start()
+    for dj, gg in peers:
+        slot = 2 * dj + gg
         pltpu.make_async_remote_copy(
             src_ref=new_buf.at[slot], dst_ref=new_buf.at[slot],
             send_sem=n_send.at[0], recv_sem=n_recv.at[slot], device_id=other, device_id_type=MESH,
         ).wait_recv()
     x_copy(1).wait_recv()
 
+    def block_at(p):
+        return look(p, [i for i, _ in at_steps]) + 2 * source(look(p, [j for _, j in at_steps]))
+
     def step(p, carry):
         later = lax.rem(p + 1, steps)
-        qb = look(p, qb_of)
-        qa_later = look(later, qa_of)
         kind_x = look(p, [int(k == "X") for k in kinds])
+        ends_block = look(p, [int(q in FINISH) for q in range(steps)]) == 1
+        done = block_at(p)
+        done_state = look(p, [state_of(i, j) for i, j in at_steps])
+
+        spare = jnp.where(ends_block, done, own)
+        finish_math(done, done_state, spare, spare)
         top_a = m0[0:1, :] * scale
-        both(qb, 1, s1, m1, s0, m0, 0, acc_a)
+        both(qb_at(p), 1, s1, m1, s0, m0, 0, acc_a)
         total_a = acc_a[hd : hd + 1, :]
         ea = top_a + log2(total_a)
         res[2 * p, 0:hd, :] = (acc_a[0:hd, :] * (1.0 / total_a)).astype(jnp.bfloat16)
         res[2 * p, hd : hd + EXT, :] = pack_log(ea)
-
-        for at, js in FORWARD.items():
-            if js:
-
-                @pl.when(p == at)
-                def _(js=js):
-                    for j in js:
-                        for i in (1, 0):
-                            q_wait(2 * j + i)
-                            forward_copy(2 * j + i).start()
-
-        for at in range(steps - 1):
-            kind, j = ORDER[at + 1]
-            if kind in "XZ":
-
-                @pl.when(p == at)
-                def _(slot=qb_of[at + 1]):
-                    q_wait(slot)
-
         top_b = m1[0:1, :] * scale
-        both(qa_later, 0, s0, m0, s1, m1, 1, acc_b)
+        both(qa_at(later), 0, s0, m0, s1, m1, 1, acc_b)
         total_b = acc_b[hd : hd + 1, :]
         eb = top_b + log2(total_b)
         ea = ea + jnp.where(kind_x == 1, NEG, 0.0)
@@ -402,14 +416,50 @@
         def _():
             r_copy(p).start()
 
-        lax.fori_loop(look(p, begins), look(p, ends), finish_block, 0)
+        @pl.when(ends_block)
+        def _():
+            finish_send(done)
+
+        @pl.when(look(p, [int(at in FORWARD) for at in range(steps)]) == 1)
+        def _():
+            entries = [FORWARD.get(at, (0, 0)) for at in range(steps)]
+            slot = 2 * source(look(p, [j for j, _ in entries])) + look(p, [i for _, i in entries])
+            q_wait(slot)
+            forward_copy(slot).start()
+
+        @pl.when(p == 1)
+        def _():
+            q_copy(ny - 1, 1).start()
+            q_copy(1, 0).start()
+
+        @pl.when(look(p, [int(k == "X") for k in kinds[1:]] + [0]) == 1)
+        def _():
+            q_wait(qb_at(p + 1))
+
+        @pl.when(look(p, [int(k == "Z") for k in kinds[2:]] + [0, 0]) == 1)
+        def _():
+            q_wait(qa_at(p + 2))
+
+        @pl.when(look(p, [int(q + 1 in FINISH) for q in range(steps)]) == 1)
+        def _():
+            r_wait(block_at(p + 1))
+
         return carry
 
     lax.fori_loop(0, steps, step, 0)
 
-    for n, (dj, di) in enumerate(peers):
-        q_copy(n, dj, di).wait_send()
-        n_copy(n, dj, di).wait_send()
+    def last(n, carry):
+        slot = look(n, [i for i, _ in FINISH_LAST]) + 2 * source(look(n, [j for _, j in FINISH_LAST]))
+        r_wait(slot)
+        finish_math(slot, look(n, [state_of(i, j) for i, j in FINISH_LAST]), slot, slot)
+        finish_send(slot)
+        return carry
+
+    lax.fori_loop(0, len(FINISH_LAST), last, 0)
+
+    for dj, gg in peers:
+        q_copy(dj, gg).wait_send()
+        n_copy(dj, gg).wait_send()
     for i in range(2):
         z_copy(i).wait_send()
         x_copy(i).wait_send()
@@ -434,8 +484,8 @@
         else:
             o_remote(slot, tile, yy).wait_send()
             l_remote(slot, tile, yy).wait_send()
-    for dj, di in peers:
-        gg, yy = peer(dj, di)
+    for dj, gg in peers:
+        yy = row(dj)
         block = 2 * yy + gg
         pltpu.make_async_remote_copy(
             src_ref=o_stage.at[0], dst_ref=o_out.at[:, heads_of(gg, yy), :],
@@ -445,6 +495,28 @@
             src_ref=lse_stage.at[0], dst_ref=lse_out.at[block],
             send_sem=l_send.at[0], recv_sem=l_recv.at[block], device_id=other, device_id_type=MESH,
         ).wait_recv()
+
+
+def last_kernel(tok, grp, o_in, lse_in, o_out, lse_out, sem):
+    copy = pltpu.make_async_copy(o_in, o_out, sem)
+    copy.start()
+    blocks, _, rows = lse_in.shape
+    token = lax.broadcasted_iota(jnp.int32, (tok, rows), 0)
+    owner = lax.div(lax.broadcasted_iota(jnp.int32, (tok, rows), 1), grp)
+    head = lax.rem(lax.broadcasted_iota(jnp.int32, (rows, blocks * grp), 0), grp)
+    column = lax.broadcasted_iota(jnp.int32, (rows, blocks * grp), 1)
+    out = None
+    for block in range(blocks):
+        spread = jnp.where(token == owner, lse_in[block, 0:1, :], 0.0)
+        place = (column == head + block * grp).astype(jnp.bfloat16)
+        hi = spread.astype(jnp.bfloat16)
+        rest = spread - hi.astype(jnp.float32)
+        mid = rest.astype(jnp.bfloat16)
+        low = (rest - mid.astype(jnp.float32)).astype(jnp.bfloat16)
+        part = dot(hi, place, 1, 0) + (dot(mid, place, 1, 0) + dot(low, place, 1, 0))
+        out = part if out is None else out + part
+    lse_out[...] = out
+    copy.wait()
 
 
 def body(queries, cache_keys, cache_values, new_keys, new_values, counts):
@@ -471,13 +543,13 @@
             vmem((2, cap, hd), bf16), vmem((2, hd + EXT, cap), bf16),
             vmem((cap, hd), bf16), vmem((hd + EXT, cap), bf16),
             vmem((2 * own, tok, grp, hd), bf16),
-            vmem((2, tok * nh, hd), bf16), vmem((own - 1, 2, tok, hd), bf16), vmem((own, 2, tok, hd), bf16),
+            vmem((2, tok * nh, hd), bf16), vmem((own, 2, tok, hd), bf16), vmem((own, 2, tok, hd), bf16),
             vmem((cap, rows), f32), vmem((cap, rows), f32), vmem((8, rows), f32), vmem((8, rows), f32),
             vmem((cap, rows // 2), bf16), vmem((cap, rows // 2), bf16),
             vmem((hd + EXT, rows), f32), vmem((hd + EXT, rows), f32),
-            vmem((2 * steps, hd + EXT, rows), bf16), vmem((own, hd + EXT, rows), bf16),
-            vmem((own, tok, grp, hd), bf16), vmem((own, 8, rows), f32),
-            dma((4,)), dma((own - 1,)), dma((2 * own,)), dma((2,)), dma((own,)), dma((own - 1,)), dma((own,)),
+            vmem((2 * steps, hd + EXT, rows), bf16), vmem((own + 1, hd + EXT, rows), bf16),
+            vmem((own + 1, tok, grp, hd), bf16), vmem((own + 1, 8, rows), f32),
+            dma((4,)), dma((own,)), dma((2 * own,)), dma((2,)), dma((own,)), dma((own,)), dma((own,)),
             dma((2,)), dma((2,)), dma((own,)), dma((own,)), dma((own,)), dma((own,)), dma((own,)), dma((own,)),
         ],
         compiler_params=pltpu.CompilerParams(
@@ -487,8 +559,13 @@
         counts, queries, cache_keys.reshape(cap * kvl, hd), cache_values.reshape(cap * kvl, hd),
         new_keys.reshape(tok * nh, hd), new_values.reshape(tok * nh, hd),
     )
-    logsum = lse[:, 0, :].reshape(own, tok, grp).transpose(1, 0, 2).reshape(tok, nq)
-    return attended, logsum
+    return pl.pallas_call(
+        functools.partial(last_kernel, tok, grp),
+        out_shape=(jax.ShapeDtypeStruct((tok, nq, hd), bf16), jax.ShapeDtypeStruct((tok, nq), f32)),
+        in_specs=[pl.BlockSpec(memory_space=vmem)] * 2,
+        out_specs=(any_space, pl.BlockSpec(memory_space=vmem)),
+        scratch_shapes=[dma],
+    )(attended, lse)
 
 
 def solution(mesh):

time: 77.2 us -> 64.7 us (0.84)
  the two profiles are of different devices: /device:TPU:1 before, /device:TPU:8 now
where the time goes in v2:
time: 64.7 us; the launch traced here: 64.6 us
  Pallas kernels  63.3 us (98%)
  between operations  1.29 us (2%)
    pallas_call x1, Pallas kernels, body(): pl.pallas_call(functools.partial(kernel, nb, ny), out_shape=(jax.ShapeDty...  60.5 us
    pallas_call x1, Pallas kernels, body(): pl.pallas_call(functools.partial(last_kernel, tok, grp), out_shape=(jax.S...  2.81 us

profile of v2, /device:TPU:8, one launch (start us, length us, event | category | flops | bytes accessed | tf_op | source)
XLA Modules:
  0.0 64.6 jit_solution(2822563844856902126)
XLA Ops:
  1.3 60.5 %shard_map.77 = (bf16[32,128,128]{2,1,0:T(8,128)(2,1)}, f32[8,8,512]{2,1,0:T(8,128)}) custom-call(s32[1]{0:T(128)S(6)} %copy.8.counts, bf16[32,128,128]{2,1,0:T(8,128)(2,1)} %q_in.1, bf16[4096,128]{1,0:T(8,128)(2,1)} %bitcast.4, bf16[4096,128]{1,0:T(8,128)(2,1)} %bitcast.5, bf16[256,128]{1,0:T(8,128)(2,1)} %bitcast.6, bf16[256,128]{1,0:T(8,128)(2,1)} %bitcast.7), custom_call_target="tpu_custom_call" | custom-call | tf_op jit(solution)/shard_map/pallas_call | solution.py:533
  61.8 2.8 %shard_map.78 = (bf16[32,128,128]{2,1,0:T(8,128)(2,1)}, f32[32,128]{1,0:T(8,128)}) custom-call(bf16[32,128,128]{2,1,0:T(8,128)(2,1)} %get-tuple-element.4.o_in, f32[8,8,512]{2,1,0:T(8,128)} %get-tuple-element.5.lse_in), custom_call_target="tpu_custom_call" | custom-call | tf_op jit(solution)/shard_map/pallas_call | solution.py:562

commit v3 on v2

--- a/solution.py
+++ b/solution.py
@@ -12,6 +12,7 @@
 LOG2E = math.log2(math.e)
 NEG = -1e30
 KC = 256
+BETWEEN = 4
 EXT = 16
 
 ORDER = (
@@ -53,7 +54,7 @@
     counts, q_in, ck_in, cv_in, nk_in, nv_in,
     o_out, lse_out,
     raw_k, raw_v, wide, k_buf, v_buf, k_send, v_send, qall, new_raw, new_send, new_buf,
-    s0, s1, m0, m1, p0, p1, acc_a, acc_b, res, part_in, o_stage, lse_stage,
+    s0, s1, m0, m1, p0, p1, acc_a, acc_b, dead, res, part_in, o_stage, lse_stage,
     load_sem, q_send, q_recv, z_send, f_send, n_send, n_recv, x_send, x_recv,
     r_send, r_recv, o_send, o_recv, l_send, l_recv,
 ):
@@ -130,6 +131,29 @@
     for base in (prev0, next0):
         for i in range(2):
             pl.semaphore_signal(barrier, inc=1, device_id=(base + i, y), device_id_type=MESH)
+
+    nh = new_raw.shape[1] // tok
+
+    def n_copy(dj, gg):
+        slot = ((ny - dj) % ny) * 2 + g
+        n = 2 * dj + gg
+        return pltpu.make_async_remote_copy(
+            src_ref=new_send.at[n], dst_ref=new_buf.at[slot],
+            send_sem=n_send.at[n], recv_sem=n_recv.at[slot],
+            device_id=(chip0 + gg, row(dj)), device_id_type=MESH,
+        )
+
+    load_nk.wait()
+    load_nv.wait()
+    for kind in range(2):
+        wide[kind * tok * nh : (kind + 1) * tok * nh, :] = new_raw[kind].astype(jnp.float32)
+    for kind in range(2):
+        for dj in range(ny):
+            for gg in range(2):
+                head = 2 * row(dj) + gg
+                x = wide[pl.ds(kind * tok * nh + head, tok, stride=nh), :].astype(jnp.bfloat16)
+                new_send[2 * dj + gg, kind] = x
+        new_buf[g, kind] = new_send[g, kind]
 
     live = counts[0]
 
@@ -158,6 +182,21 @@
         return carry
 
     lax.fori_loop(0, cap // KC, split_keys, 0)
+    pl.semaphore_wait(barrier, len(peers) + 4)
+    x_copy(0).start()
+    q_copy(0, 1 - g).start()
+
+    @pl.when(g == 1)
+    def _():
+        z_copy(0).start()
+        z_copy(1).start()
+
+    for dj, gg in peers:
+        n_copy(dj, gg).start()
+
+    q_copy(ny - 1, 0).start()
+    q_copy(1, 1).start()
+
     load_v.wait()
 
     def split_values(c, carry):
@@ -180,44 +219,7 @@
 
     lax.fori_loop(0, cap // KC, split_values, 0)
 
-    nh = new_raw.shape[1] // tok
-
-    def n_copy(dj, gg):
-        slot = ((ny - dj) % ny) * 2 + g
-        n = 2 * dj + gg
-        return pltpu.make_async_remote_copy(
-            src_ref=new_send.at[n], dst_ref=new_buf.at[slot],
-            send_sem=n_send.at[n], recv_sem=n_recv.at[slot],
-            device_id=(chip0 + gg, row(dj)), device_id_type=MESH,
-        )
-
-    load_nk.wait()
-    load_nv.wait()
-    for kind in range(2):
-        wide[kind * tok * nh : (kind + 1) * tok * nh, :] = new_raw[kind].astype(jnp.float32)
-    for kind in range(2):
-        for dj in range(ny):
-            for gg in range(2):
-                head = 2 * row(dj) + gg
-                x = wide[pl.ds(kind * tok * nh + head, tok, stride=nh), :].astype(jnp.bfloat16)
-                new_send[2 * dj + gg, kind] = x
-        new_buf[g, kind] = new_send[g, kind]
-
-    pl.semaphore_wait(barrier, len(peers) + 4)
-    x_copy(0).start()
-    q_copy(0, 1 - g).start()
-
-    @pl.when(g == 1)
-    def _():
-        z_copy(0).start()
-        z_copy(1).start()
-
     x_copy(1).start()
-    for dj, gg in peers:
-        n_copy(dj, gg).start()
-
-    q_copy(ny - 1, 0).start()
-    q_copy(1, 1).start()
 
     def scores(qa, t, seg, kk):
         qq = qall[qa, t * (tok // 2) : (t + 1) * (tok // 2)].reshape(half, hd)
@@ -237,20 +239,29 @@
                 top = fold(s) if top is None else jnp.maximum(top, fold(s))
             m_ref[:, cols] = jnp.broadcast_to(jnp.max(top, axis=0, keepdims=True), (8, half))
 
-    def both(qa, seg, s_new, m_new, s_old, m_old, seg_old, acc):
-        for t in range(2):
-            cols = slice(t * half, (t + 1) * half)
-            p_ref = (p0, p1)[t]
-            old = m_old[0:1, cols]
-            top = None
-            for c in range(cap // KC):
-                kk = slice(c * KC, (c + 1) * KC)
-                s = scores(qa, t, seg, kk)
-                s_new[kk, cols] = s
-                top = fold(s) if top is None else jnp.maximum(top, fold(s))
-                p_ref[kk, :] = jnp.exp2((s_old[kk, cols] - old) * scale).astype(jnp.bfloat16)
-            m_new[:, cols] = jnp.broadcast_to(jnp.max(top, axis=0, keepdims=True), (8, half))
-            acc[:, cols] = dot(v_buf[seg_old], p_ref[...], 1, 0)
+    def tile(t, qa, seg, s_new, m_new, s_old, m_old, seg_old, between):
+        cols = slice(t * half, (t + 1) * half)
+        p_ref = (p0, p1)[t]
+        old = m_old[0:1, cols] * scale
+        top = total = None
+        for c in range(cap // KC):
+            if c == BETWEEN:
+                between()
+            kk = slice(c * KC, (c + 1) * KC)
+            s = scores(qa, t, seg, kk)
+            s_new[kk, cols] = s
+            top = fold(s) if top is None else jnp.maximum(top, fold(s))
+            p = jnp.exp2(s_old[kk, cols] * scale - old)
+            p_ref[kk, :] = p.astype(jnp.bfloat16)
+            if c == 0:
+                weight_0 = p[0:1, :]
+            part = jnp.sum(p.reshape(KC // 8, 8, half), axis=0) - dead[seg_old, c] * weight_0
+            total = part if total is None else total + part
+        m_new[:, cols] = jnp.broadcast_to(jnp.max(top, axis=0, keepdims=True), (8, half))
+        return jnp.sum(total, axis=0, keepdims=True)
+
+    def mix_half(t, seg, acc):
+        acc[:, t * half : (t + 1) * half] = dot(v_buf[seg, 0:hd], (p0, p1)[t][...], 1, 0)
 
     def log2(x):
         return jnp.log(x) * LOG2E
@@ -268,6 +279,9 @@
 
     def qb_at(p):
         return look(p, base_b) + 2 * source(look(p, sources))
+
+    def seg_at(p):
+        return g * look(p, [int(k != "X") for k in kinds])
 
     at_steps = [FINISH.get(p, (0, 0)) for p in range(steps)]
 
@@ -362,8 +376,7 @@
 
     load_q.wait()
     q_wait(1 - g)
-    x_copy(0).wait_recv()
-    first(qa_at(0), 0, s0, m0)
+    first(qa_at(0), seg_at(0), s0, m0)
 
     @pl.when(g == 0)
     def _():
@@ -379,7 +392,13 @@
             src_ref=new_buf.at[slot], dst_ref=new_buf.at[slot],
             send_sem=n_send.at[0], recv_sem=n_recv.at[slot], device_id=other, device_id_type=MESH,
         ).wait_recv()
+    x_copy(0).wait_recv()
     x_copy(1).wait_recv()
+    for seg in range(2):
+        for c in range(cap // KC):
+            marks = v_buf[seg, hd : hd + EXT, c * KC : (c + 1) * KC].astype(jnp.float32)
+            rows_live = jnp.sum(jnp.sum(marks, axis=0, keepdims=True), axis=1, keepdims=True)
+            dead[seg, c] = jnp.broadcast_to((KC - rows_live) * 0.125, (8, half))
 
     def block_at(p):
         return look(p, [i for i, _ in at_steps]) + 2 * source(look(p, [j for _, j in at_steps]))
@@ -392,23 +411,28 @@
         done_state = look(p, [state_of(i, j) for i, j in at_steps])
 
         spare = jnp.where(ends_block, done, own)
-        finish_math(done, done_state, spare, spare)
         top_a = m0[0:1, :] * scale
-        both(qb_at(p), 1, s1, m1, s0, m0, 0, acc_a)
-        total_a = acc_a[hd : hd + 1, :]
+        qb, qa = qb_at(p), qa_at(later)
+        seg_a, seg_later = seg_at(p), seg_at(later)
+        seg_b = 1 - seg_a
+        a0 = tile(0, qb, seg_b, s1, m1, s0, m0, seg_a, lambda: finish_math(done, done_state, spare, spare))
+        a1 = tile(1, qb, seg_b, s1, m1, s0, m0, seg_a, lambda: mix_half(0, seg_a, acc_a))
+        top_b = m1[0:1, :] * scale
+        b0 = tile(0, qa, seg_later, s0, m0, s1, m1, seg_b, lambda: mix_half(1, seg_a, acc_a))
+        b1 = tile(1, qa, seg_later, s0, m0, s1, m1, seg_b, lambda: mix_half(0, seg_b, acc_b))
+        mix_half(1, seg_b, acc_b)
+        total_a = jnp.concatenate([a0, a1], axis=1)
         ea = top_a + log2(total_a)
-        res[2 * p, 0:hd, :] = (acc_a[0:hd, :] * (1.0 / total_a)).astype(jnp.bfloat16)
+        res[2 * p, 0:hd, :] = (acc_a[...] * (1.0 / total_a)).astype(jnp.bfloat16)
         res[2 * p, hd : hd + EXT, :] = pack_log(ea)
-        top_b = m1[0:1, :] * scale
-        both(qa_at(later), 0, s0, m0, s1, m1, 1, acc_b)
-        total_b = acc_b[hd : hd + 1, :]
+        total_b = jnp.concatenate([b0, b1], axis=1)
         eb = top_b + log2(total_b)
         ea = ea + jnp.where(kind_x == 1, NEG, 0.0)
         high = jnp.maximum(ea, eb)
         wa = jnp.exp2(ea - high)
         wb = jnp.exp2(eb - high)
         whole = wa + wb
-        merged = acc_a[0:hd, :] * (wa / (whole * total_a)) + acc_b[0:hd, :] * (wb / (whole * total_b))
+        merged = acc_a[...] * (wa / (whole * total_a)) + acc_b[...] * (wb / (whole * total_b))
         res[2 * p + 1, 0:hd, :] = merged.astype(jnp.bfloat16)
         res[2 * p + 1, hd : hd + EXT, :] = pack_log(high + log2(whole))
 
@@ -513,8 +537,8 @@
         rest = spread - hi.astype(jnp.float32)
         mid = rest.astype(jnp.bfloat16)
         low = (rest - mid.astype(jnp.float32)).astype(jnp.bfloat16)
-        part = dot(hi, place, 1, 0) + (dot(mid, place, 1, 0) + dot(low, place, 1, 0))
-        out = part if out is None else out + part
+        piece = dot(hi, place, 1, 0) + (dot(mid, place, 1, 0) + dot(low, place, 1, 0))
+        out = piece if out is None else out + piece
     lse_out[...] = out
     copy.wait()
 
@@ -546,7 +570,7 @@
             vmem((2, tok * nh, hd), bf16), vmem((own, 2, tok, hd), bf16), vmem((own, 2, tok, hd), bf16),
             vmem((cap, rows), f32), vmem((cap, rows), f32), vmem((8, rows), f32), vmem((8, rows), f32),
             vmem((cap, rows // 2), bf16), vmem((cap, rows // 2), bf16),
-            vmem((hd + EXT, rows), f32), vmem((hd + EXT, rows), f32),
+            vmem((hd, rows), f32), vmem((hd, rows), f32), vmem((2, cap // KC, 8, rows // 2), f32),
             vmem((2 * steps, hd + EXT, rows), bf16), vmem((own + 1, hd + EXT, rows), bf16),
             vmem((own + 1, tok, grp, hd), bf16), vmem((own + 1, 8, rows), f32),
             dma((4,)), dma((own,)), dma((2 * own,)), dma((2,)), dma((own,)), dma((own,)), dma((own,)),

time: 64.7 us -> 64.1 us (level)
  no operation moved by 1% of the time
where the time goes in v3:
time: 64.1 us; the launch traced here: 64 us
  Pallas kernels  62.7 us (98%)
  between operations  1.29 us (2%)
    pallas_call x1, Pallas kernels, body(): pl.pallas_call(functools.partial(kernel, nb, ny), out_shape=(jax.ShapeDty...  59.9 us
    pallas_call x1, Pallas kernels, body(): pl.pallas_call(functools.partial(last_kernel, tok, grp), out_shape=(jax.S...  2.81 us

profile of v3, /device:TPU:8, one launch (start us, length us, event | category | flops | bytes accessed | tf_op | source)
XLA Modules:
  0.0 64.0 jit_solution(8247486684371589692)
XLA Ops:
  1.3 59.9 %shard_map.77 = (bf16[32,128,128]{2,1,0:T(8,128)(2,1)}, f32[8,8,512]{2,1,0:T(8,128)}) custom-call(s32[1]{0:T(128)S(6)} %copy.8.counts, bf16[32,128,128]{2,1,0:T(8,128)(2,1)} %q_in.1, bf16[4096,128]{1,0:T(8,128)(2,1)} %bitcast.4, bf16[4096,128]{1,0:T(8,128)(2,1)} %bitcast.5, bf16[256,128]{1,0:T(8,128)(2,1)} %bitcast.6, bf16[256,128]{1,0:T(8,128)(2,1)} %bitcast.7), custom_call_target="tpu_custom_call" | custom-call | tf_op jit(solution)/shard_map/pallas_call | solution.py:557
  61.2 2.8 %shard_map.78 = (bf16[32,128,128]{2,1,0:T(8,128)(2,1)}, f32[32,128]{1,0:T(8,128)}) custom-call(bf16[32,128,128]{2,1,0:T(8,128)(2,1)} %get-tuple-element.4.o_in, f32[8,8,512]{2,1,0:T(8,128)} %get-tuple-element.5.lse_in), custom_call_target="tpu_custom_call" | custom-call | tf_op jit(solution)/shard_map/pallas_call | solution.py:586

commit v4 on v3

--- a/solution.py
+++ b/solution.py
@@ -21,7 +21,7 @@
 )
 FINISH = {4: (1, 0), 6: (0, 0), 7: (1, 1), 8: (0, 1), 9: (1, 2), 10: (0, 2)}
 FINISH_LAST = ((1, 3), (0, 3))
-FORWARD = {0: (1, 1), 1: (1, 0), 2: (2, 1), 3: (2, 0), 5: (3, 1), 6: (3, 0)}
+FORWARD = {0: (1, 1), 1: (1, 0), 3: (2, 1), 4: (2, 0), 5: (3, 1), 6: (3, 0)}
 
 
 def look(position, values):
@@ -451,7 +451,7 @@
             q_wait(slot)
             forward_copy(slot).start()
 
-        @pl.when(p == 1)
+        @pl.when(p == 2)
         def _():
             q_copy(ny - 1, 1).start()
             q_copy(1, 0).start()

time: 64.1 us -> 67.5 us (1.053)
  Pallas kernels: 62.7 us -> 66.1 us
    pallas_call x1, Pallas kernels: 59.9 us -> 63.3 us  [body(): pl.pallas_call(functools.partial(kernel, nb, ny), out_shape=(jax.ShapeDty...]
where the time goes in v4:
time: 67.5 us; the launch traced here: 67.4 us
  Pallas kernels  66.1 us (98%)
  between operations  1.29 us (2%)
    pallas_call x1, Pallas kernels, body(): pl.pallas_call(functools.partial(kernel, nb, ny), out_shape=(jax.ShapeDty...  63.3 us
    pallas_call x1, Pallas kernels, body(): pl.pallas_call(functools.partial(last_kernel, tok, grp), out_shape=(jax.S...  2.81 us

profile of v4, /device:TPU:8, one launch (start us, length us, event | category | flops | bytes accessed | tf_op | source)
XLA Modules:
  0.0 67.4 jit_solution(6442717373385732249)
XLA Ops:
  1.3 63.3 %shard_map.77 = (bf16[32,128,128]{2,1,0:T(8,128)(2,1)}, f32[8,8,512]{2,1,0:T(8,128)}) custom-call(s32[1]{0:T(128)S(6)} %copy.8.counts, bf16[32,128,128]{2,1,0:T(8,128)(2,1)} %q_in.1, bf16[4096,128]{1,0:T(8,128)(2,1)} %bitcast.4, bf16[4096,128]{1,0:T(8,128)(2,1)} %bitcast.5, bf16[256,128]{1,0:T(8,128)(2,1)} %bitcast.6, bf16[256,128]{1,0:T(8,128)(2,1)} %bitcast.7), custom_call_target="tpu_custom_call" | custom-call | tf_op jit(solution)/shard_map/pallas_call | solution.py:557
  64.6 2.8 %shard_map.78 = (bf16[32,128,128]{2,1,0:T(8,128)(2,1)}, f32[32,128]{1,0:T(8,128)}) custom-call(bf16[32,128,128]{2,1,0:T(8,128)(2,1)} %get-tuple-element.4.o_in, f32[8,8,512]{2,1,0:T(8,128)} %get-tuple-element.5.lse_in), custom_call_target="tpu_custom_call" | custom-call | tf_op jit(solution)/shard_map/pallas_call | solution.py:586
